TPU v7x, 1024 devices: a whole 4x8x16 slice. The times are simulated.
1024 devices in a mesh: dp: 64 (over x, y, core), own: 16 (over z).
Axes of the slice: x: 4, y: 8, z: 16, core: 2. Of those that a mesh axis runs over, the one named last changes fastest.
Arguments:
- embeddings: bfloat16 [131072, 4096], P(('dp', 'own')), may hold values from -16 to 16
- coarse_ids: int32 [131072], P(('dp', 'own')), may hold values from 0 to 255, as said below
- fine_cents: bfloat16 [16384, 4096], P('dp'), may hold values from -3 to 3
- coarse_prev: bfloat16 [256, 4096], P('dp'), may hold values from -3 to 3
Outputs:
- fine_next: float32 [16384, 4096], P('dp', 'own')
- weight_totals: float32 [16384], P('dp')
- coarse_next: bfloat16 [256, 4096], replicated
Inputs may be any that keep to these rules, and one draw needn't show every extreme that they name: `coarse_ids`: cluster c belongs to owner group c // 4. Within the 128 rows of one device, at most 4 rows name clusters of any one owner group, and some owner group is named by exactly 4 of them.
All inputs are finite; a program needn't handle non-finite values.
Results may differ from a plain program's by a relative error of at most 0.013.
Values may be sent and summed in bfloat16 or wider, within the bound.
A program may use at most 32 MiB of HBM per device.

v0:
```python
import math

import jax
import jax.numpy as jnp
from jax import lax
from jax.sharding import PartitionSpec as P

FINE_PER = 64
CLU_DEV = 4


def on_device(embeddings, coarse_ids, fine_cents, coarse_prev):
    rows, width = embeddings.shape
    n_dp = lax.axis_size("dp")
    n_own = lax.axis_size("own")
    capacity = 2 * rows // n_dp
    group_fines = fine_cents.shape[0]
    scale = 4.0 / math.sqrt(width)
    owner = coarse_ids // CLU_DEV
    hits = (owner[:, None] == jnp.arange(n_dp, dtype=jnp.int32)[None, :]).astype(jnp.int32)
    rank = jnp.sum(jnp.cumsum(hits, axis=0) * hits, axis=1) - 1
    place = owner * capacity + rank
    outbox = (
        jnp.zeros((n_dp * capacity, width), jnp.bfloat16)
        .at[place]
        .set(embeddings)
        .reshape(n_dp, capacity, width)
    )
    labels = (
        jnp.full((n_dp * capacity,), -1, jnp.int32)
        .at[place]
        .set(coarse_ids)
        .reshape(n_dp, capacity)
    )
    first_cluster = lax.axis_index("dp") * CLU_DEV
    fsq = jnp.sum(jnp.square(fine_cents.astype(jnp.float32)), axis=1)
    cluster_of = (jnp.arange(group_fines, dtype=jnp.int32) // FINE_PER)[None, :]
    cluster_ids = jnp.arange(CLU_DEV, dtype=jnp.int32)[None, :]
    inbox, tags = (
        lax.all_to_all(outbox, "dp", split_axis=0, concat_axis=0, tiled=True),
        lax.all_to_all(labels, "dp", split_axis=0, concat_axis=0, tiled=True),
    )
    flat = inbox.reshape(-1, width)
    flat_tags = tags.reshape(-1)
    valid = flat_tags >= 0
    local = jnp.where(valid, flat_tags - first_cluster, 0)
    pick = (local[:, None] == cluster_ids).astype(jnp.bfloat16)
    base = jnp.dot(pick, coarse_prev, preferred_element_type=jnp.float32)
    resid = (flat.astype(jnp.float32) - base).astype(jnp.bfloat16)
    prod = lax.dot_general(
        resid, fine_cents, (((1,), (1,)), ((), ())), preferred_element_type=jnp.float32
    )
    logits = (prod - 0.5 * fsq[None, :]) * scale
    logits = jnp.where(cluster_of == local[:, None], logits, jnp.float32(-1e30))
    top = jnp.max(logits, axis=1, keepdims=True)
    expo = jnp.exp(logits - top)
    probs = expo / jnp.sum(expo, axis=1, keepdims=True) * valid[:, None].astype(jnp.float32)
    probs, resid = (probs, resid)
    weights = probs.astype(jnp.bfloat16)
    stats = lax.dot_general(
        weights, resid, (((0,), (0,)), ((), ())), preferred_element_type=jnp.float32
    )
    totals = lax.psum(jnp.sum(probs, axis=0), "own")
    shares = lax.psum_scatter(
        stats.astype(jnp.bfloat16), "own", scatter_dimension=1, tiled=True
    ).astype(jnp.float32)
    columns = width // n_own
    column_start = lax.axis_index("own") * columns
    fine_part = lax.dynamic_slice_in_dim(fine_cents, column_start, columns, 1).astype(jnp.float32)
    fine_next = (4.0 * fine_part + shares) / (4.0 + totals[:, None])
    coarse_part = lax.dynamic_slice_in_dim(coarse_prev, column_start, columns, 1).astype(
        jnp.float32
    )
    coarse_piece = (
        coarse_part + jnp.mean(fine_next.reshape(CLU_DEV, FINE_PER, columns), axis=1)
    ).astype(jnp.bfloat16)
    group_rows = lax.all_gather(coarse_piece, "own", axis=1, tiled=True)
    coarse_next = lax.all_gather(group_rows, "dp", axis=0, tiled=True)
    return (fine_next, totals, coarse_next)


def solution(mesh):
    placed = (P(("dp", "own"), None), P(("dp", "own")), P("dp", None), P("dp", None))
    return jax.shard_map(
        on_device,
        mesh=mesh,
        in_specs=placed,
        out_specs=(P("dp", "own"), P("dp"), P()),
        check_vma=False,
    )
```

profile of v0, /device:TPU:1, one launch (start us, length us, event | category | flops | bytes accessed | tf_op | source)
XLA Modules:
  0.0 312.6 jit_solution(13961157328570210602)
XLA Ops:
  7.2 0.7 and_select_fusion
  7.9 0.2 reduce_window_sum.11
  8.1 0.2 select_reduce_fusion
  8.3 0.7 compare_select_fusion.1
  8.9 1.1 scatter_custom_fusion
  10.1 0.7 all_to_all.9
  10.8 18.2 %all-to-all-start = ((s32[64,1,4]{2,1,0:T(1,128)}), s32[64,1,4]{2,1,0:T(1,128)S(1)}, u32[]{:S(2)}, u32[]{:S(2)}) async-start(s32[64,1,4]{2,1,0:T(1,128)} %bitcast), calls=%async_computation | async-start | bytes 65536 | tf_op jit(solution)/shard_map/all_to_all | solution.py:41
  29.0 3.4 %scatter_custom_fusion.1 = bf16[256,4096]{1,0:T(8,128)(2,1)S(1)} fusion(s32[128]{0:T(128)S(1)} %compare_select_fusion.1, bf16[128,4096]{1,0:T(8,128)(2,1)} %param.4, bf16[]{:T(256)} %constant.68.clone.1), kind=kCustom, calls=%fused_computation.9 | custom fusion | bytes 2097664 | tf_op jit(solution)/shard_map/scatter | solution.py:26
  32.4 2.2 reshape.67
  34.6 3.7 %all-to-all-done = s32[64,1,4]{2,1,0:T(1,128)S(1)} async-done(((s32[64,1,4]{2,1,0:T(1,128)}), s32[64,1,4]{2,1,0:T(1,128)S(1)}, u32[]{:S(2)}, u32[]{:S(2)}) %all-to-all-start) | async-done | bytes 1056 | tf_op jit(solution)/shard_map/all_to_all | solution.py:41
  38.3 6.7 %all-to-all-start.1 = ((bf16[64,4,4096]{2,1,0:T(4,128)(2,1)}), bf16[64,4,4096]{2,1,0:T(4,128)(2,1)S(1)}, u32[]{:S(2)}, u32[]{:S(2)}) async-start(bf16[64,4,4096]{2,1,0:T(4,128)(2,1)} %reshape.67), calls=%async_computation.1 | async-start | bytes 4194304 | tf_op jit(solution)/shard_map/all_to_all | solution.py:40
  45.1 2.1 multiply_reduce_fusion
  47.6 48.6 %all-to-all-done.1 = bf16[64,4,4096]{2,1,0:T(4,128)(2,1)S(1)} async-done(((bf16[64,4,4096]{2,1,0:T(4,128)(2,1)}), bf16[64,4,4096]{2,1,0:T(4,128)(2,1)S(1)}, u32[]{:S(2)}, u32[]{:S(2)}) %all-to-all-start.1) | async-done | bytes 2097184 | tf_op jit(solution)/shard_map/all_to_all | solution.py:40
  96.3 2.5 reshape.69
  98.8 3.1 fusion
  101.9 0.8 fusion.14
  102.7 2.0 convolution_convert_fusion
  104.8 0.1 fusion.9
  104.9 29.9 %psum.7 = f32[256]{0:T(256)S(1)} all-reduce(f32[256]{0:T(256)S(1)} %fusion.9), channel_id=1, replica_groups=mesh['dp'=64,'own'=16] {'own'}, use_global_device_ids=true, to_apply=%region_9.10 | all-reduce | flops 256 | bytes 2048 | tf_op jit(solution)/shard_map/psum | solution.py:63
  134.8 33.6 %reduce-scatter.2.cloned.1.call-done = bf16[256,256]{1,0:T(8,128)(2,1)} async-done(((bf16[256,4096]{1,0:T(8,128)(2,1)}), bf16[256,256]{1,0:T(8,128)(2,1)}) %reduce-scatter.2.cloned.1.call-update) | async-done | bytes 131088 | tf_op jit(solution)/shard_map/reduce_scatter | solution.py:64
  168.5 1.7 bitcast_reduce_fusion
  170.2 23.1 %all_gather.6 = bf16[4,4096]{1,0:T(4,128)(2,1)} all-gather(bf16[4,256]{1,0:T(4,128)(2,1)S(1)} %add_convert_fusion), channel_id=1, replica_groups=mesh['dp'=64,'own'=16] {'own'}, dimensions={1}, use_global_device_ids=true | all-gather | bytes 34816 | tf_op jit(solution)/shard_map/all_gather | solution.py:77
  193.3 108.5 %all-gather.3.cloned.1.call-done = bf16[64,4,4096]{2,1,0:T(4,128)(2,1)} async-done(((bf16[1,4,4096]{2,1,0:T(4,128)(2,1)}), bf16[64,4,4096]{2,1,0:T(4,128)(2,1)}) %all-gather.3.cloned.1.call-update) | async-done | bytes 2097168 | tf_op jit(solution)/shard_map/all_gather | solution.py:78
  301.8 3.9 %reshape.90 = bf16[256,4096]{1,0:T(8,128)(2,1)} reshape(bf16[64,4,4096]{2,1,0:T(4,128)(2,1)} %all-gather.3.cloned.1.call-done) | data formatting | bytes 4194304
  (20 shorter events, 0.7 us)
Async XLA Ops:
  10.8 27.5 %all-to-all-start = ((s32[64,1,4]{2,1,0:T(1,128)}), s32[64,1,4]{2,1,0:T(1,128)S(1)}, u32[]{:S(2)}, u32[]{:S(2)}) async-start(s32[64,1,4]{2,1,0:T(1,128)} %bitcast), calls=%async_computation | async-start | bytes 65536 | tf_op jit(solution)/shard_map/all_to_all | solution.py:41
  38.3 58.0 %all-to-all-start.1 = ((bf16[64,4,4096]{2,1,0:T(4,128)(2,1)}), bf16[64,4,4096]{2,1,0:T(4,128)(2,1)S(1)}, u32[]{:S(2)}, u32[]{:S(2)}) async-start(bf16[64,4,4096]{2,1,0:T(4,128)(2,1)} %reshape.67), calls=%async_computation.1 | async-start | bytes 4194304 | tf_op jit(solution)/shard_map/all_to_all | solution.py:40
  45.0 123.4 %reduce-scatter.2.cloned.1.call-start = ((), (), s32[]{:S(2)}) async-start(), calls=%async_computation.3 | async-start | bytes 2228224 | tf_op jit(solution)/shard_map/reduce_scatter | solution.py:64
  47.6 51.1 %copy-start.1 = (bf16[4,4096]{1,0:T(4,128)(2,1)S(1)}, bf16[4,4096]{1,0:T(4,128)(2,1)}, u32[]{:S(2)}) copy-start(bf16[4,4096]{1,0:T(4,128)(2,1)} %param.7) | copy-start | bytes 98308
  98.8 3.1 copy-start
  104.8 197.0 %all-gather.3.cloned.1.call-start = ((), (), s32[]{:S(2)}) async-start(), calls=%async_computation.4 | async-start | bytes 2129920 | tf_op jit(solution)/shard_map/all_gather | solution.py:78
  134.8 170.9 %copy-start.2 = (f32[256]{0:T(256)}, f32[256]{0:T(256)S(1)}, u32[]{:S(2)}) copy-start(f32[256]{0:T(256)S(1)} %psum.7) | copy-start | bytes 3076
Sparse Core Ops, SparseCore 0:
  104.9 63.5 reduce-scatter.1
  193.4 108.3 all-gather.2
where the time goes:
time: 313 us
  waiting for transfers between devices  195 us (62%)
  blocking collectives  52.9 us (17%)
  starting transfers between devices  25 us (8%)
  between operations  14.2 us (5%)
  local copies, waits for them, and re-layouts  14.1 us (5%)
  other arithmetic  6.01 us (2%)
  matrix products  5.88 us (2%)
    all_gather x1, waiting for transfers between devices, on_device(): coarse_next = lax.all_gather(group_rows, 'dp', axis=0, tiled=True)  109 us
    all_to_all x1, waiting for transfers between devices, on_device(): lax.all_to_all(outbox, 'dp', split_axis=0, concat_axis=0, tiled=True)  48.6 us
    reduce_scatter x1, waiting for transfers between devices, on_device(): lax.psum_scatter(stats.astype(jnp.bfloat16), 'own', scatter_dimension=1,...  33.6 us
    psum x1, blocking collectives, on_device(): totals = lax.psum(jnp.sum(probs, axis=0), 'own')  29.9 us
    all_gather x1, blocking collectives, on_device(): group_rows = lax.all_gather(coarse_piece, 'own', axis=1, tiled=True)  23.1 us
    all_to_all x1, starting transfers between devices, on_device(): lax.all_to_all(labels, 'dp', split_axis=0, concat_axis=0, tiled=True)  18.2 us
    all_to_all x1, starting transfers between devices, on_device(): lax.all_to_all(outbox, 'dp', split_axis=0, concat_axis=0, tiled=True)  6.74 us
  transfers between devices with their start and end apart: 4, of which 4 were waited for; matrix products, arithmetic and copies ran while one was open for 3% of the time, Pallas kernels for 0%

commit v1 on v0

v1 whole, which is shorter than its diff:
```python
import functools
import math

import jax
import jax.numpy as jnp
from jax import lax
from jax.experimental import pallas as pl
from jax.experimental.pallas import tpu as pltpu
from jax.sharding import PartitionSpec as P

MESH = pl.DeviceIdType.MESH
FINE_PER = 64
CLU_DEV = 4
CAP = 4
PARTS = 4
BLK = CAP * PARTS
N_X = 4
SUBS = 2
F32 = jnp.float32
BF16 = jnp.bfloat16


def drain(ref, sem):
    pltpu.make_async_copy(ref, ref, sem).wait()


def iota(shape, dim):
    return lax.broadcasted_iota(jnp.int32, shape, dim)


def kernel(
    n_x,
    n_y,
    n_z,
    emb_hbm,
    ids_ref,
    fines_hbm,
    coarse_ref,
    fine_out,
    tot_out,
    coarse_out,
    emb,
    fines,
    outbox,
    inbox,
    ids_box,
    ids_f,
    resid,
    stats,
    rs_src,
    rs_buf,
    tot_box,
    cpart,
    cbox,
    zbox,
    own_piece,
    block,
    agbuf,
    load_sem,
    ids_send,
    ids_recv,
    a2a_send,
    a2a_recv,
    rs_send,
    rs_recv,
    st_send,
    st_recv,
):
    n_dp = 2 * n_x * n_y
    rows, width = emb_hbm.shape
    part = width // PARTS
    group_fines = fines.shape[0]
    cols = width // n_z
    n_h = cols // 128
    scale = 4.0 / math.sqrt(width)

    me = lax.axis_index("dp")
    z = lax.axis_index("own")
    core = lax.rem(me, 2)
    chip = lax.div(me, 2)
    y = lax.rem(chip, n_y)
    x = lax.div(chip, n_y)

    def send(src, dst, send_sem, recv_sem, **to):
        copy = pltpu.make_async_remote_copy(
            src_ref=src,
            dst_ref=dst,
            send_sem=send_sem,
            recv_sem=recv_sem,
            device_id=to,
            device_id_type=MESH,
        )
        copy.start()

    def z_peers(body):
        @pl.loop(1, n_z)
        def _(k):
            body(lax.rem(z + k, n_z))

    barrier = pltpu.get_barrier_semaphore()

    loads = []
    for p in range(PARTS):
        loads.append(
            pltpu.make_async_copy(
                emb_hbm.at[:, pl.ds(p * part, part)],
                emb.at[pl.ds(p * rows, rows)],
                load_sem.at[p],
            )
        )
    loads.append(pltpu.make_async_copy(fines_hbm, fines, load_sem.at[PARTS]))
    for load in loads:
        load.start()

    @pl.loop(1, n_dp)
    def _(k):
        pl.semaphore_signal(
            barrier, inc=1, device_id={"dp": lax.rem(me + k, n_dp)}, device_id_type=MESH
        )

    @pl.loop(1, n_z)
    def _(k):
        pl.semaphore_signal(
            barrier, inc=1, device_id={"own": lax.rem(z + k, n_z)}, device_id_type=MESH
        )

    ids = ids_ref[0]
    owner = ids >> 2
    owner_rows = jnp.broadcast_to(owner.astype(F32), (rows, rows))
    eye = iota((rows, rows), 0) == iota((rows, rows), 1)
    before = iota((rows, rows), 0) < iota((rows, rows), 1)
    owner_col = jnp.sum(jnp.where(eye, owner_rows, 0.0), axis=1, keepdims=True)
    same = jnp.where(before & (owner_col == owner_rows), 1.0, 0.0)
    rank = jnp.sum(same, axis=0, keepdims=True).astype(jnp.int32)
    y_bits = n_y.bit_length() - 1
    to_core = owner & 1
    to_y = (owner >> 1) & (n_y - 1)
    to_x = owner >> (1 + y_bits)
    dxi = (to_x - x + 2 * n_x - 1) & (n_x - 1)
    dy = (to_y - y + n_y) & (n_y - 1)
    half = n_y // 2
    dyi = jnp.where(dy >= half, 2 * (dy - half), 2 * (half - dy) - 1)
    place = ((to_core * n_x + dxi) * n_y + dyi) * BLK + rank
    target = jnp.concatenate([place + p * CAP for p in range(PARTS)], axis=1)

    ids_box[n_dp - 2] = ids
    for load in loads[:PARTS]:
        load.wait()
    pl.semaphore_wait(barrier, n_dp - 1 + n_z - 1)

    chunk = n_y * BLK

    @pl.loop(0, 2 * n_x)
    def _(jc):
        base = pl.multiple_of(jc * chunk, chunk)
        hot = (iota((chunk, PARTS * rows), 0) + base == target).astype(F32).astype(BF16)
        outbox[pl.ds(base, chunk), :] = jnp.dot(
            hot, emb[...], preferred_element_type=F32
        ).astype(BF16)
        dest_core = lax.div(jc, n_x)
        at_x = lax.rem(jc, n_x)
        dest_x = lax.rem(x + at_x + 1, n_x)
        flip = lax.rem(dest_core + core, 2)
        for at_y in range(n_y):
            step = (at_y + 1) // 2
            delta = (n_y // 2 + (step if at_y % 2 == 0 else -step)) % n_y
            dest = (dest_x * n_y + lax.rem(y + delta, n_y)) * 2 + dest_core
            slot = (at_x * n_y + at_y) * 2 + flip
            src = outbox.at[pl.ds(pl.multiple_of(base + at_y * BLK, BLK), BLK)]
            dst = inbox.at[pl.ds(pl.multiple_of(slot * BLK, BLK), BLK)]

            def post():
                send(ids_ref.at[0], ids_box.at[slot], ids_send, ids_recv, dp=dest)
                send(src, dst, a2a_send, a2a_recv.at[at_x], dp=dest)

            if at_y < n_y - 1:
                post()
            else:
                mine = (at_x == n_x - 1) & (flip == 0)
                pl.when(jnp.logical_not(mine))(post)

                @pl.when(mine)
                def _():
                    pltpu.make_async_copy(src, dst, a2a_recv.at[at_x]).start()

    loads[PARTS].wait()
    fsq_col = jnp.sum(jnp.square(fines[...].astype(F32)), axis=1, keepdims=True)
    eye_f = iota((group_fines, group_fines), 0) == iota((group_fines, group_fines), 1)
    fsq = jnp.sum(jnp.where(eye_f, fsq_col, 0.0), axis=0, keepdims=True)

    drain(ids_box.at[pl.ds(0, n_dp - 1)], ids_recv)
    for i in range(n_dp):
        ids_f[pl.ds(i, 1), :] = ids_box[i].astype(F32)
    slots = n_dp * CAP
    spread = (iota((slots, n_dp), 0) >> 2) == iota((slots, n_dp), 1)
    seen = jnp.dot(
        spread.astype(F32).astype(BF16), ids_f[...].astype(BF16), preferred_element_type=F32
    )
    low = (me * CLU_DEV).astype(F32)
    ours = jnp.where((seen >= low) & (seen < low + CLU_DEV), 1.0, 0.0)
    order = jnp.dot(
        ours.astype(BF16), before.astype(F32).astype(BF16), preferred_element_type=F32
    )
    nth = (iota((slots, rows), 0) & (CAP - 1)).astype(F32)
    tag = jnp.sum(
        jnp.where(order == nth, ours * (seen - low + 1.0), 0.0), axis=1, keepdims=True
    )

    src_b = 2 * n_y
    rows_b = src_b * CAP
    out_row = iota((src_b * BLK, src_b * BLK), 0)
    in_row = iota((src_b * BLK, src_b * BLK), 1)
    quarter = lax.div(out_row, rows_b)
    within = lax.rem(out_row, rows_b)
    perm = (in_row == (within >> 2) * BLK + quarter * CAP + (within & 3)).astype(F32).astype(BF16)
    for b in range(n_x):
        arrived = inbox.at[pl.ds(b * src_b * BLK, src_b * BLK)]
        drain(arrived, a2a_recv.at[b])
        flat = jnp.dot(perm, arrived[...], preferred_element_type=F32)
        tag_b = tag[b * rows_b : (b + 1) * rows_b]
        for p in range(PARTS):
            prev = jnp.zeros((rows_b, part), F32)
            for c in range(CLU_DEV):
                row = coarse_ref[pl.ds(c, 1), pl.ds(p * part, part)].astype(F32)
                prev = jnp.where(tag_b == c + 1.0, row, prev)
            resid[pl.ds(b * rows_b, rows_b), pl.ds(p * part, part)] = (
                flat[p * rows_b : (p + 1) * rows_b] - prev
            ).astype(BF16)

    prod = lax.dot_general(
        resid[...], fines[...], (((1,), (1,)), ((), ())), preferred_element_type=F32
    )
    logits = (prod - 0.5 * fsq) * scale
    cluster_of = (iota((1, group_fines), 1) >> 6).astype(F32) + 1.0
    logits = jnp.where(cluster_of == tag, logits, -1e30)
    top = jnp.max(logits, axis=1, keepdims=True)
    expo = jnp.exp(logits - top)
    valid = jnp.where(tag > 0.0, 1.0, 0.0)
    probs = expo / jnp.sum(expo, axis=1, keepdims=True) * valid

    tot_box[z] = jnp.sum(probs, axis=0, keepdims=True)
    z_peers(
        lambda to: send(tot_box.at[z], tot_box.at[z], st_send.at[0], st_recv.at[0], own=to)
    )

    weights = jnp.transpose(probs).astype(BF16)

    def chunk_stats(to):
        at = pl.multiple_of(to * cols, 128)
        return jnp.dot(weights, resid[:, pl.ds(at, cols)], preferred_element_type=F32)

    steps = (n_z // 2, n_z - 1 - n_z // 2)
    sub = group_fines // SUBS

    def target_of(way, t):
        off = steps[0] - t if way == 0 else n_z - steps[1] + t
        return lax.rem(z + off, n_z)

    def ring_send(way, t, s, src):
        to = lax.rem(z + (1 if way == 0 else n_z - 1), n_z)
        send(
            src,
            rs_buf.at[way, t, pl.ds(s * sub, sub)],
            rs_send.at[way, t, s],
            rs_recv.at[way, t, s],
            own=to,
        )

    def ring_first():
        for way in range(2):
            if steps[way] > 0:
                rs_src[way] = chunk_stats(target_of(way, 0)).astype(BF16)
                for s in range(SUBS):
                    ring_send(way, 0, s, rs_src.at[way, pl.ds(s * sub, sub)])

    def ring_step(t):
        for s in range(SUBS):
            for way in range(2):
                if t >= steps[way]:
                    continue
                held = rs_buf.at[way, t - 1, pl.ds(s * sub, sub)]
                drain(held, rs_recv.at[way, t - 1, s])
                add = stats[target_of(way, t), pl.ds(s * sub, sub), :]
                held[...] = (held[...].astype(F32) + add).astype(BF16)
                ring_send(way, t, s, held)

    ring_first()

    @pl.loop(0, n_z)
    def _(to):
        stats[to] = chunk_stats(to)

    ring_step(1)

    if n_z > 1:
        drain(tot_box.at[pl.ds(0, n_z - 1)], st_recv.at[0])
    totals = tot_box[0]
    for k in range(1, n_z):
        totals = totals + tot_box[k]
    tot_out[...] = totals
    tot_col = jnp.sum(jnp.where(eye_f, totals, 0.0), axis=1, keepdims=True)
    share = 1.0 / (4.0 + tot_col)
    mean_share = share * (1.0 / FINE_PER)

    def put(ref, value):
        for h in range(n_h):
            ref[pl.ds(h * CLU_DEV, CLU_DEV), :] = value[:, h * 128 : (h + 1) * 128]

    def cluster_sum(value):
        return jnp.sum(value.reshape(CLU_DEV, FINE_PER, cols), axis=1)

    @pl.loop(0, n_z)
    def _(to):
        put(cpart.at[to], cluster_sum(stats[to] * mean_share))

    cbox[z] = cpart[z]
    z_peers(
        lambda to: send(cpart.at[to], cbox.at[z], st_send.at[1], st_recv.at[1], own=to)
    )
    my_cols = pl.ds(pl.multiple_of(z * cols, 128), cols)
    fine_part = fines[:, my_cols].astype(F32)
    put(
        own_piece,
        coarse_ref[:, my_cols].astype(F32) + cluster_sum(4.0 * fine_part * mean_share),
    )
    ring_step(2)

    if n_z > 1:
        drain(cbox.at[pl.ds(0, n_z - 1)], st_recv.at[1])
    piece = own_piece[...]
    for k in range(n_z):
        piece = piece + cbox[k]
    zbox[z] = piece
    z_peers(
        lambda to: send(zbox.at[z], zbox.at[z], st_send.at[2], st_recv.at[2], own=to)
    )
    ring_step(3)

    if n_z > 1:
        drain(zbox.at[pl.ds(0, n_z - 1)], st_recv.at[2])
    for k in range(n_z):
        got = zbox[k]
        for h in range(n_h):
            at = k * cols + h * 128
            block[pl.ds(at // part * CLU_DEV, CLU_DEV), pl.ds(at % part, 128)] = got[
                h * CLU_DEV : (h + 1) * CLU_DEV
            ]
    agbuf[core, y] = block[...].astype(BF16)

    @pl.loop(1, n_y)
    def _(k):
        dest = (x * n_y + lax.rem(y + k, n_y)) * 2 + core
        send(agbuf.at[core, y], agbuf.at[core, y], st_send.at[3], st_recv.at[3], dp=dest)

    ring_step(4)
    if n_y > 1:
        drain(agbuf.at[0, pl.ds(0, n_y - 1)], st_recv.at[3])
    other = me + 1 - 2 * core
    send(agbuf.at[core], agbuf.at[core], st_send.at[4], st_recv.at[4], dp=other)
    ring_step(5)
    drain(agbuf.at[0], st_recv.at[4])
    rows_x = 2 * n_y * CLU_DEV
    within_y = lax.div(within, 2 * CLU_DEV)
    within_core = (within >> 2) & 1
    from_row = (within_core * n_y + within_y) * BLK + quarter * CAP + (within & 3)
    perm_x = (in_row == from_row).astype(F32).astype(BF16)
    gathered = jnp.dot(
        perm_x, agbuf[...].reshape(2 * n_y * BLK, part), preferred_element_type=F32
    ).astype(BF16)
    own_rows = pl.ds(pl.multiple_of(x * rows_x, rows_x), rows_x)
    for p in range(PARTS):
        coarse_out[own_rows, pl.ds(p * part, part)] = gathered[p * rows_x : (p + 1) * rows_x]
    half_cols = pl.ds(pl.multiple_of(core * (width // 2), 128), width // 2)
    mine_x = coarse_out.at[own_rows, half_cols]

    @pl.loop(1, n_x)
    def _(k):
        dest = (lax.rem(x + k, n_x) * n_y + y) * 2 + core
        send(mine_x, mine_x, st_send.at[5], st_recv.at[5], dp=dest)

    ring_step(6)
    others = coarse_out.at[pl.ds(0, rows_x * (n_x - 1)), pl.ds(0, width // 2)]
    drain(others, st_recv.at[5])

    @pl.loop(1, n_x)
    def _(k):
        at_rows = pl.ds(pl.multiple_of(lax.rem(x + k, n_x) * rows_x, rows_x), rows_x)
        view = coarse_out.at[at_rows, half_cols]
        send(view, view, st_send.at[6], st_recv.at[6], dp=other)

    for t in range(7, steps[0]):
        ring_step(t)

    sums = stats[z]
    for way in range(2):
        if steps[way] > 0:
            for s in range(SUBS):
                last = steps[way] - 1
                drain(rs_buf.at[way, last, pl.ds(s * sub, sub)], rs_recv.at[way, last, s])
            sums = sums + rs_buf[way, steps[way] - 1].astype(F32)
    fine_out[...] = (4.0 * fine_part + sums) * share

    drain(others, st_recv.at[6])
    drain(ids_box.at[pl.ds(0, n_dp - 1)], ids_send)
    drain(outbox.at[pl.ds(0, (n_dp - 1) * BLK)], a2a_send)
    if n_z > 1:
        drain(tot_box.at[pl.ds(0, n_z - 1)], st_send.at[0])
        drain(cbox.at[pl.ds(0, n_z - 1)], st_send.at[1])
        drain(zbox.at[pl.ds(0, n_z - 1)], st_send.at[2])
    if n_y > 1:
        drain(agbuf.at[0, pl.ds(0, n_y - 1)], st_send.at[3])
    drain(agbuf.at[0], st_send.at[4])
    drain(others, st_send.at[5])
    drain(others, st_send.at[6])
    for way in range(2):
        for t in range(steps[way]):
            for s in range(SUBS):
                drain(rs_buf.at[way, t, pl.ds(s * sub, sub)], rs_send.at[way, t, s])


def solution(mesh):
    n_dp, n_z = mesh.shape["dp"], mesh.shape["own"]
    n_x = N_X
    n_y = n_dp // (2 * n_x)

    def on_device(embeddings, coarse_ids, fine_cents, coarse_prev):
        rows, width = embeddings.shape
        group_fines = fine_cents.shape[0]
        cols = width // n_z
        part = width // PARTS
        lanes = cols // 128 * CLU_DEV
        vmem = pl.BlockSpec(memory_space=pltpu.VMEM)
        hbm = pl.BlockSpec(memory_space=pl.ANY)
        dma = pltpu.SemaphoreType.DMA
        fine_next, totals, coarse_next = pl.pallas_call(
            functools.partial(kernel, n_x, n_y, n_z),
            out_shape=(
                jax.ShapeDtypeStruct((group_fines, cols), F32),
                jax.ShapeDtypeStruct((1, group_fines), F32),
                jax.ShapeDtypeStruct((n_dp * CLU_DEV, width), BF16),
            ),
            in_specs=[hbm, vmem, hbm, vmem],
            out_specs=(vmem, vmem, vmem),
            scratch_shapes=[
                pltpu.VMEM((PARTS * rows, part), BF16),
                pltpu.VMEM((group_fines, width), BF16),
                pltpu.VMEM((n_dp * BLK, part), BF16),
                pltpu.VMEM((n_dp * BLK, part), BF16),
                pltpu.VMEM((n_dp, 1, rows), jnp.int32),
                pltpu.VMEM((n_dp, rows), F32),
                pltpu.VMEM((n_dp * CAP, width), BF16),
                pltpu.VMEM((n_z, group_fines, cols), F32),
                pltpu.VMEM((2, group_fines, cols), BF16),
                pltpu.VMEM((2, max(n_z // 2, 1), group_fines, cols), BF16),
                pltpu.VMEM((n_z, 1, group_fines), F32),
                pltpu.VMEM((n_z, lanes, 128), F32),
                pltpu.VMEM((n_z, lanes, 128), F32),
                pltpu.VMEM((n_z, lanes, 128), F32),
                pltpu.VMEM((lanes, 128), F32),
                pltpu.VMEM((BLK, part), F32),
                pltpu.VMEM((2, n_y, BLK, part), BF16),
                dma((PARTS + 1,)),
                dma(()),
                dma(()),
                dma(()),
                dma((n_x,)),
                dma((2, max(n_z // 2, 1), SUBS)),
                dma((2, max(n_z // 2, 1), SUBS)),
                dma((7,)),
                dma((7,)),
            ],
            compiler_params=pltpu.CompilerParams(
                collective_id=0, has_side_effects=True, vmem_limit_bytes=48 * 2**20
            ),
        )(embeddings, coarse_ids.reshape(1, 1, rows), fine_cents, coarse_prev)
        return fine_next, totals.reshape(group_fines), coarse_next

    placed = (P(("dp", "own"), None), P(("dp", "own")), P("dp", None), P("dp", None))
    return jax.shard_map(
        on_device,
        mesh=mesh,
        in_specs=placed,
        out_specs=(P("dp", "own"), P("dp"), P()),
        check_vma=False,
    )
```

time: 313 us -> 129 us (0.41)
  waiting for transfers between devices: 195 us -> 0 us
  Pallas kernels: 0 us -> 120 us
  blocking collectives: 52.9 us -> 0 us
  starting transfers between devices: 25 us -> 0 us
  between operations: 14.2 us -> 0.65 us
  local copies, waits for them, and re-layouts: 14.1 us -> 6.81 us
  other arithmetic: 6.01 us -> 0 us
  matrix products: 5.88 us -> 0 us
    pallas_call x0 -> x1, Pallas kernels: none -> 120 us  [on_device(): pl.pallas_call(functools.partial(kernel, n_x, n_y, n_z), out_shape=(jax.S...]
    all_gather x1 -> x0, waiting for transfers between devices: 109 us -> none  [on_device(): coarse_next = lax.all_gather(group_rows, 'dp', axis=0, tiled=True)]
    all_to_all x2 -> x0, waiting for transfers between devices: 52.3 us -> none  [the longest x1 48.6 us: on_device(): lax.all_to_all(outbox, 'dp', split_axis=0, concat_axis=0, tiled=True)]
    reduce_scatter x1 -> x0, waiting for transfers between devices: 33.6 us -> none  [on_device(): lax.psum_scatter(stats.astype(jnp.bfloat16), 'own', scatter_dimension=1,...]
    psum x1 -> x0, blocking collectives: 29.9 us -> none  [on_device(): totals = lax.psum(jnp.sum(probs, axis=0), 'own')]
    all_to_all x2 -> x0, starting transfers between devices: 24.9 us -> none  [the longest x1 18.2 us: on_device(): lax.all_to_all(labels, 'dp', split_axis=0, concat_axis=0, tiled=True)]
    all_gather x1 -> x0, blocking collectives: 23.1 us -> none  [on_device(): group_rows = lax.all_gather(coarse_piece, 'own', axis=1, tiled=True)]
    dot_general x3 -> x0, matrix products: 5.88 us -> none  [the longest x1 3.08 us: on_device(): base = jnp.dot(pick, coarse_prev, preferred_element_type=jnp.float32)]
  transfers between devices with their start and end apart: 4 -> 0, of which waited for: 4 -> 0; matrix products, arithmetic and copies ran while one was open for 3% -> 0% of each run, Pallas kernels for 0% -> 0%
where the time goes in v1:
time: 129 us; the launch traced here: 128 us
  Pallas kernels  120 us (93%)
  local copies, waits for them, and re-layouts  6.81 us (5%)
    pallas_call x1, Pallas kernels, on_device(): pl.pallas_call(functools.partial(kernel, n_x, n_y, n_z), out_shape=(jax.S...  120 us
    unnamed x11, local copies, waits for them, and re-layouts  6.81 us

profile of v1, /device:TPU:1, one launch (start us, length us, event | category | flops | bytes accessed | tf_op | source)
XLA Modules:
  0.0 127.6 jit_solution(12605542092271240151)
XLA Ops:
  0.6 0.0 copy-start
  0.6 1.6 %copy-done = bf16[256,4096]{1,0:T(8,128)(2,1)S(1)} copy-done((bf16[256,4096]{1,0:T(8,128)(2,1)S(1)}, bf16[256,4096]{1,0:T(8,128)(2,1)}, u32[]{:S(2)}) %copy-start) | copy-done | bytes 2097176
  2.2 0.0 copy-start.1
  2.2 1.2 copy-done.1
  3.4 0.0 copy-start.2
  3.5 0.8 copy-done.2
  4.2 0.0 copy-start.3
  4.2 0.7 copy-done.3
  4.9 120.2 %shard_map.67 = (f32[256,256]{1,0:T(8,128)S(1)}, f32[1,256]{1,0:T(1,128)S(1)}, bf16[256,4096]{1,0:T(8,128)(2,1)S(1)}) custom-call(bf16[128,4096]{1,0:T(8,128)(2,1)S(1)} %copy-done.1, s32[1,1,128]{2,1,0:T(1,128)S(1)} %bitcast.3, bf16[256,4096]{1,0:T(8,128)(2,1)S(1)} %copy-done, bf16[4,4096]{1,0:T(4,128)(2,1)S(1)} %copy-done.2), custom_call_target="tpu_custom_call" | custom-call | tf_op jit(solution)/shard_map/pallas_call | solution.py:435
  125.0 0.7 copy.10
  125.7 0.6 copy.11
  126.3 1.3 %copy.12 = bf16[256,4096]{1,0:T(8,128)(2,1)} copy(bf16[256,4096]{1,0:T(8,128)(2,1)S(1)} %get-tuple-element.14) | data formatting | bytes 4194304
Async XLA Ops:
  0.6 1.6 %copy-start = (bf16[256,4096]{1,0:T(8,128)(2,1)S(1)}, bf16[256,4096]{1,0:T(8,128)(2,1)}, u32[]{:S(2)}) copy-start(bf16[256,4096]{1,0:T(8,128)(2,1)} %fines_hbm.1) | copy-start | bytes 6291460
  2.2 1.2 copy-start.1
  3.4 0.8 copy-start.2
  4.2 0.7 copy-start.3

commit v2 on v1

--- a/solution.py
+++ b/solution.py
@@ -33,29 +33,33 @@
     n_y,
     n_z,
     emb_hbm,
+    ids_hbm,
+    fines_hbm,
+    coarse_hbm,
+    fine_hbm,
+    tot_hbm,
+    blocks_hbm,
+    emb,
     ids_ref,
-    fines_hbm,
+    fines,
     coarse_ref,
-    fine_out,
-    tot_out,
-    coarse_out,
-    emb,
-    fines,
     outbox,
     inbox,
     ids_box,
     ids_f,
     resid,
+    prod_box,
     stats,
     rs_src,
     rs_buf,
     tot_box,
     cpart,
     cbox,
-    zbox,
-    own_piece,
-    block,
-    agbuf,
+    folded,
+    mine_y,
+    gath,
+    fine_out,
+    tot_out,
     load_sem,
     ids_send,
     ids_recv,
@@ -65,13 +69,16 @@
     rs_recv,
     st_send,
     st_recv,
+    y_recv,
+    x_recv,
+    core_recv,
+    store_sem,
 ):
     n_dp = 2 * n_x * n_y
     rows, width = emb_hbm.shape
     part = width // PARTS
     group_fines = fines.shape[0]
     cols = width // n_z
-    n_h = cols // 128
     scale = 4.0 / math.sqrt(width)
 
     me = lax.axis_index("dp")
@@ -109,6 +116,9 @@
             )
         )
     loads.append(pltpu.make_async_copy(fines_hbm, fines, load_sem.at[PARTS]))
+    loads.append(pltpu.make_async_copy(coarse_hbm, coarse_ref, load_sem.at[PARTS + 1]))
+    load_ids = pltpu.make_async_copy(ids_hbm, ids_ref, load_sem.at[PARTS + 2])
+    load_ids.start()
     for load in loads:
         load.start()
 
@@ -124,6 +134,7 @@
             barrier, inc=1, device_id={"own": lax.rem(z + k, n_z)}, device_id_type=MESH
         )
 
+    load_ids.wait()
     ids = ids_ref[0]
     owner = ids >> 2
     owner_rows = jnp.broadcast_to(owner.astype(F32), (rows, rows))
@@ -184,6 +195,7 @@
                     pltpu.make_async_copy(src, dst, a2a_recv.at[at_x]).start()
 
     loads[PARTS].wait()
+    loads[PARTS + 1].wait()
     fsq_col = jnp.sum(jnp.square(fines[...].astype(F32)), axis=1, keepdims=True)
     eye_f = iota((group_fines, group_fines), 0) == iota((group_fines, group_fines), 1)
     fsq = jnp.sum(jnp.where(eye_f, fsq_col, 0.0), axis=0, keepdims=True)
@@ -226,10 +238,14 @@
             resid[pl.ds(b * rows_b, rows_b), pl.ds(p * part, part)] = (
                 flat[p * rows_b : (p + 1) * rows_b] - prev
             ).astype(BF16)
-
-    prod = lax.dot_general(
-        resid[...], fines[...], (((1,), (1,)), ((), ())), preferred_element_type=F32
-    )
+        prod_box[pl.ds(b * rows_b, rows_b), :] = lax.dot_general(
+            resid[pl.ds(b * rows_b, rows_b), :],
+            fines[...],
+            (((1,), (1,)), ((), ())),
+            preferred_element_type=F32,
+        )
+
+    prod = prod_box[...]
     logits = (prod - 0.5 * fsq) * scale
     cluster_of = (iota((1, group_fines), 1) >> 6).astype(F32) + 1.0
     logits = jnp.where(cluster_of == tag, logits, -1e30)
@@ -285,111 +301,102 @@
                 ring_send(way, t, s, held)
 
     ring_first()
-
-    @pl.loop(0, n_z)
-    def _(to):
-        stats[to] = chunk_stats(to)
-
+    wide = part // cols
+    for p in range(PARTS):
+        quarter_stats = jnp.dot(
+            weights, resid[:, pl.ds(p * part, part)], preferred_element_type=F32
+        )
+        for k in range(wide):
+            stats[p * wide + k] = quarter_stats[:, k * cols : (k + 1) * cols]
     ring_step(1)
-
-    if n_z > 1:
-        drain(tot_box.at[pl.ds(0, n_z - 1)], st_recv.at[0])
+    ring_step(2)
+
+    drain(tot_box.at[pl.ds(0, n_z - 1)], st_recv.at[0])
     totals = tot_box[0]
     for k in range(1, n_z):
         totals = totals + tot_box[k]
     tot_out[...] = totals
+    store_tot = pltpu.make_async_copy(tot_out, tot_hbm, store_sem.at[0])
+    store_tot.start()
     tot_col = jnp.sum(jnp.where(eye_f, totals, 0.0), axis=1, keepdims=True)
     share = 1.0 / (4.0 + tot_col)
     mean_share = share * (1.0 / FINE_PER)
 
-    def put(ref, value):
-        for h in range(n_h):
-            ref[pl.ds(h * CLU_DEV, CLU_DEV), :] = value[:, h * 128 : (h + 1) * 128]
-
     def cluster_sum(value):
         return jnp.sum(value.reshape(CLU_DEV, FINE_PER, cols), axis=1)
 
-    @pl.loop(0, n_z)
-    def _(to):
-        put(cpart.at[to], cluster_sum(stats[to] * mean_share))
-
-    cbox[z] = cpart[z]
-    z_peers(
-        lambda to: send(cpart.at[to], cbox.at[z], st_send.at[1], st_recv.at[1], own=to)
-    )
-    my_cols = pl.ds(pl.multiple_of(z * cols, 128), cols)
-    fine_part = fines[:, my_cols].astype(F32)
-    put(
-        own_piece,
-        coarse_ref[:, my_cols].astype(F32) + cluster_sum(4.0 * fine_part * mean_share),
-    )
-    ring_step(2)
-
-    if n_z > 1:
-        drain(cbox.at[pl.ds(0, n_z - 1)], st_recv.at[1])
-    piece = own_piece[...]
+    for p in range(PARTS):
+        for k in range(wide):
+            folded[pl.ds(k * CLU_DEV, CLU_DEV), :] = cluster_sum(stats[p * wide + k] * mean_share)
+        cpart[p] = folded[...].astype(BF16)
+    my_quarter = lax.rem(z, PARTS)
+    cbox[z] = cpart[my_quarter]
+    for d in range(1, n_z):
+        to = lax.rem(z + d, n_z)
+        send(cpart.at[lax.rem(to, PARTS)], cbox.at[z], st_send.at[1], st_recv.at[1], own=to)
+    for k in range(wide):
+        at = pl.ds(pl.multiple_of(my_quarter * part + k * cols, 128), cols)
+        folded[pl.ds(k * CLU_DEV, CLU_DEV), :] = coarse_ref[:, at].astype(F32) + cluster_sum(
+            4.0 * fines[:, at].astype(F32) * mean_share
+        )
+    ring_step(3)
+    ring_step(4)
+
+    drain(cbox.at[pl.ds(0, n_z - 1)], st_recv.at[1])
+    piece = folded[...]
     for k in range(n_z):
-        piece = piece + cbox[k]
-    zbox[z] = piece
-    z_peers(
-        lambda to: send(zbox.at[z], zbox.at[z], st_send.at[2], st_recv.at[2], own=to)
-    )
-    ring_step(3)
-
-    if n_z > 1:
-        drain(zbox.at[pl.ds(0, n_z - 1)], st_recv.at[2])
-    for k in range(n_z):
-        got = zbox[k]
-        for h in range(n_h):
-            at = k * cols + h * 128
-            block[pl.ds(at // part * CLU_DEV, CLU_DEV), pl.ds(at % part, 128)] = got[
-                h * CLU_DEV : (h + 1) * CLU_DEV
-            ]
-    agbuf[core, y] = block[...].astype(BF16)
-
-    @pl.loop(1, n_y)
-    def _(k):
-        dest = (x * n_y + lax.rem(y + k, n_y)) * 2 + core
-        send(agbuf.at[core, y], agbuf.at[core, y], st_send.at[3], st_recv.at[3], dp=dest)
-
-    ring_step(4)
-    if n_y > 1:
-        drain(agbuf.at[0, pl.ds(0, n_y - 1)], st_recv.at[3])
+        piece = piece + cbox[k].astype(F32)
+    quarter_cols = pl.ds(pl.multiple_of(my_quarter * cols, 128), cols)
+    mine = mine_y.at[:, quarter_cols]
+    mine[...] = piece.astype(BF16)
+    for d in (1, n_z - 1, n_z - 2):
+        send(mine, mine, st_send.at[2], st_recv.at[2], own=lax.rem(z + d, n_z))
+    ring_step(5)
+    drain(mine_y.at[:, pl.ds(0, 3 * cols)], st_recv.at[2])
+
     other = me + 1 - 2 * core
-    send(agbuf.at[core], agbuf.at[core], st_send.at[4], st_recv.at[4], dp=other)
-    ring_step(5)
-    drain(agbuf.at[0], st_recv.at[4])
-    rows_x = 2 * n_y * CLU_DEV
-    within_y = lax.div(within, 2 * CLU_DEV)
-    within_core = (within >> 2) & 1
-    from_row = (within_core * n_y + within_y) * BLK + quarter * CAP + (within & 3)
-    perm_x = (in_row == from_row).astype(F32).astype(BF16)
-    gathered = jnp.dot(
-        perm_x, agbuf[...].reshape(2 * n_y * BLK, part), preferred_element_type=F32
-    ).astype(BF16)
-    own_rows = pl.ds(pl.multiple_of(x * rows_x, rows_x), rows_x)
-    for p in range(PARTS):
-        coarse_out[own_rows, pl.ds(p * part, part)] = gathered[p * rows_x : (p + 1) * rows_x]
-    half_cols = pl.ds(pl.multiple_of(core * (width // 2), 128), width // 2)
-    mine_x = coarse_out.at[own_rows, half_cols]
-
-    @pl.loop(1, n_x)
-    def _(k):
-        dest = (lax.rem(x + k, n_x) * n_y + y) * 2 + core
-        send(mine_x, mine_x, st_send.at[5], st_recv.at[5], dp=dest)
-
+    gath[core, x, y] = mine_y[...]
+    near = sorted(range(1, n_y), key=lambda k: min(k, n_y - k))
+
+    def along_x(at_y):
+        block = gath.at[core, x, at_y]
+        for k in range(1, n_x):
+            dest = (lax.rem(x + k, n_x) * n_y + y) * 2 + core
+            send(block, block, st_send.at[5], x_recv.at[k], dp=dest)
+
+    for k in near:
+        dest = (x * n_y + lax.rem(y + n_y - k, n_y)) * 2 + core
+        block = gath.at[core, x, y]
+        send(block, block, st_send.at[3], y_recv.at[k], dp=dest)
+    along_x(y)
     ring_step(6)
-    others = coarse_out.at[pl.ds(0, rows_x * (n_x - 1)), pl.ds(0, width // 2)]
-    drain(others, st_recv.at[5])
-
-    @pl.loop(1, n_x)
-    def _(k):
-        at_rows = pl.ds(pl.multiple_of(lax.rem(x + k, n_x) * rows_x, rows_x), rows_x)
-        view = coarse_out.at[at_rows, half_cols]
-        send(view, view, st_send.at[6], st_recv.at[6], dp=other)
-
+    for k in near:
+        at_y = lax.rem(y + k, n_y)
+        drain(gath.at[core, x, at_y], y_recv.at[k])
+        along_x(at_y)
+
+    def pass_on(k):
+        column = gath.at[core, lax.rem(x - k + n_x, n_x)]
+        send(column, column, st_send.at[4], core_recv.at[k], dp=other)
+        store_column(core, k, k)
+
+    stores = []
+
+    def store_column(of_core, k, sem):
+        at = lax.rem(x - k + n_x, n_x)
+        stores.append(
+            pltpu.make_async_copy(
+                gath.at[of_core, at], blocks_hbm.at[of_core, at], store_sem.at[2 + sem]
+            )
+        )
+        stores[-1].start()
+
+    pass_on(0)
     for t in range(7, steps[0]):
         ring_step(t)
+    for k in range(1, n_x):
+        drain(gath.at[core, lax.rem(x - k + n_x, n_x)], x_recv.at[k])
+        pass_on(k)
 
     sums = stats[z]
     for way in range(2):
@@ -398,24 +405,52 @@
                 last = steps[way] - 1
                 drain(rs_buf.at[way, last, pl.ds(s * sub, sub)], rs_recv.at[way, last, s])
             sums = sums + rs_buf[way, steps[way] - 1].astype(F32)
-    fine_out[...] = (4.0 * fine_part + sums) * share
-
-    drain(others, st_recv.at[6])
+    my_cols = pl.ds(pl.multiple_of(z * cols, 128), cols)
+    fine_out[...] = (4.0 * fines[:, my_cols].astype(F32) + sums) * share
+
+    store_fine = pltpu.make_async_copy(fine_out, fine_hbm, store_sem.at[1])
+    store_fine.start()
+
+    for k in range(n_x):
+        at = lax.rem(x - k + n_x, n_x)
+        drain(gath.at[1 - core, at], core_recv.at[k])
+        store_column(1 - core, k, n_x + k)
+    for store in [store_tot, store_fine, *stores]:
+        store.wait()
     drain(ids_box.at[pl.ds(0, n_dp - 1)], ids_send)
     drain(outbox.at[pl.ds(0, (n_dp - 1) * BLK)], a2a_send)
-    if n_z > 1:
-        drain(tot_box.at[pl.ds(0, n_z - 1)], st_send.at[0])
-        drain(cbox.at[pl.ds(0, n_z - 1)], st_send.at[1])
-        drain(zbox.at[pl.ds(0, n_z - 1)], st_send.at[2])
-    if n_y > 1:
-        drain(agbuf.at[0, pl.ds(0, n_y - 1)], st_send.at[3])
-    drain(agbuf.at[0], st_send.at[4])
-    drain(others, st_send.at[5])
-    drain(others, st_send.at[6])
+    drain(tot_box.at[pl.ds(0, n_z - 1)], st_send.at[0])
+    drain(cbox.at[pl.ds(0, n_z - 1)], st_send.at[1])
+    drain(mine_y.at[:, pl.ds(0, 3 * cols)], st_send.at[2])
+    drain(gath.at[0, 0, pl.ds(0, n_y - 1)], st_send.at[3])
+    drain(gath.at[0], st_send.at[4])
+    drain(gath.at[0, pl.ds(0, n_x - 1)], st_send.at[5])
     for way in range(2):
         for t in range(steps[way]):
             for s in range(SUBS):
                 drain(rs_buf.at[way, t, pl.ds(s * sub, sub)], rs_send.at[way, t, s])
+
+
+def arrange(n_y, blocks, fine, tot, fine_out, tot_out, coarse_out):
+    blk, width = blocks.shape[-2:]
+    wide = blk // CLU_DEV
+    cols = width // PARTS
+    rows_x = 2 * n_y * CLU_DEV
+    out_row = iota((rows_x * wide, rows_x * wide), 0)
+    in_row = iota((rows_x * wide, rows_x * wide), 1)
+    within = lax.rem(out_row, rows_x)
+    from_block = ((within >> 2) & 1) * n_y + lax.div(within, 2 * CLU_DEV)
+    from_row = from_block * blk + lax.div(out_row, rows_x) * CLU_DEV + (within & 3)
+    perm = (in_row == from_row).astype(F32).astype(BF16)
+    both = jnp.concatenate([blocks[c, 0, i] for c in range(2) for i in range(n_y)], axis=0)
+    rows = jnp.dot(perm, both, preferred_element_type=F32).astype(BF16)
+    for p in range(PARTS):
+        for j in range(wide):
+            coarse_out[:, pl.ds((p * wide + j) * cols, cols)] = rows[
+                j * rows_x : (j + 1) * rows_x, p * cols : (p + 1) * cols
+            ]
+    fine_out[...] = fine[...]
+    tot_out[...] = tot[...]
 
 
 def solution(mesh):
@@ -428,51 +463,80 @@
         group_fines = fine_cents.shape[0]
         cols = width // n_z
         part = width // PARTS
-        lanes = cols // 128 * CLU_DEV
-        vmem = pl.BlockSpec(memory_space=pltpu.VMEM)
+        blk = part // cols * CLU_DEV
         hbm = pl.BlockSpec(memory_space=pl.ANY)
         dma = pltpu.SemaphoreType.DMA
-        fine_next, totals, coarse_next = pl.pallas_call(
+        fine_next, totals, blocks = pl.pallas_call(
             functools.partial(kernel, n_x, n_y, n_z),
             out_shape=(
                 jax.ShapeDtypeStruct((group_fines, cols), F32),
                 jax.ShapeDtypeStruct((1, group_fines), F32),
-                jax.ShapeDtypeStruct((n_dp * CLU_DEV, width), BF16),
+                jax.ShapeDtypeStruct((2, n_x, n_y, blk, PARTS * cols), BF16),
             ),
-            in_specs=[hbm, vmem, hbm, vmem],
-            out_specs=(vmem, vmem, vmem),
+            in_specs=[hbm, hbm, hbm, hbm],
+            out_specs=(hbm, hbm, hbm),
             scratch_shapes=[
                 pltpu.VMEM((PARTS * rows, part), BF16),
+                pltpu.VMEM((1, 1, rows), jnp.int32),
                 pltpu.VMEM((group_fines, width), BF16),
+                pltpu.VMEM((CLU_DEV, width), BF16),
                 pltpu.VMEM((n_dp * BLK, part), BF16),
                 pltpu.VMEM((n_dp * BLK, part), BF16),
                 pltpu.VMEM((n_dp, 1, rows), jnp.int32),
                 pltpu.VMEM((n_dp, rows), F32),
                 pltpu.VMEM((n_dp * CAP, width), BF16),
+                pltpu.VMEM((n_dp * CAP, group_fines), F32),
                 pltpu.VMEM((n_z, group_fines, cols), F32),
                 pltpu.VMEM((2, group_fines, cols), BF16),
                 pltpu.VMEM((2, max(n_z // 2, 1), group_fines, cols), BF16),
                 pltpu.VMEM((n_z, 1, group_fines), F32),
-                pltpu.VMEM((n_z, lanes, 128), F32),
-                pltpu.VMEM((n_z, lanes, 128), F32),
-                pltpu.VMEM((n_z, lanes, 128), F32),
-                pltpu.VMEM((lanes, 128), F32),
-                pltpu.VMEM((BLK, part), F32),
-                pltpu.VMEM((2, n_y, BLK, part), BF16),
-                dma((PARTS + 1,)),
+                pltpu.VMEM((PARTS, blk, cols), BF16),
+                pltpu.VMEM((n_z, blk, cols), BF16),
+                pltpu.VMEM((blk, cols), F32),
+                pltpu.VMEM((blk, PARTS * cols), BF16),
+                pltpu.VMEM((2, n_x, n_y, blk, PARTS * cols), BF16),
+                pltpu.VMEM((group_fines, cols), F32),
+                pltpu.VMEM((1, group_fines), F32),
+                dma((PARTS + 3,)),
                 dma(()),
                 dma(()),
                 dma(()),
                 dma((n_x,)),
                 dma((2, max(n_z // 2, 1), SUBS)),
                 dma((2, max(n_z // 2, 1), SUBS)),
-                dma((7,)),
-                dma((7,)),
+                dma((6,)),
+                dma((3,)),
+                dma((n_y,)),
+                dma((n_x,)),
+                dma((n_x,)),
+                dma((2 + 2 * n_x,)),
             ],
             compiler_params=pltpu.CompilerParams(
-                collective_id=0, has_side_effects=True, vmem_limit_bytes=48 * 2**20
+                collective_id=0, has_side_effects=True, vmem_limit_bytes=60 * 2**20
             ),
         )(embeddings, coarse_ids.reshape(1, 1, rows), fine_cents, coarse_prev)
+        whole_fine = pl.BlockSpec((group_fines, cols), lambda i: (0, 0))
+        whole_tot = pl.BlockSpec((1, group_fines), lambda i: (0, 0))
+        fine_next, totals, coarse_next = pl.pallas_call(
+            functools.partial(arrange, n_y),
+            grid=(n_x,),
+            out_shape=(
+                jax.ShapeDtypeStruct((group_fines, cols), F32),
+                jax.ShapeDtypeStruct((1, group_fines), F32),
+                jax.ShapeDtypeStruct((n_dp * CLU_DEV, width), BF16),
+            ),
+            in_specs=[
+                pl.BlockSpec((2, 1, n_y, blk, PARTS * cols), lambda i: (0, i, 0, 0, 0)),
+                whole_fine,
+                whole_tot,
+            ],
+            out_specs=(
+                whole_fine,
+                whole_tot,
+                pl.BlockSpec((2 * n_y * CLU_DEV, width), lambda i: (i, 0)),
+            ),
+            compiler_params=pltpu.CompilerParams(vmem_limit_bytes=60 * 2**20),
+        )(blocks, fine_next, totals)
         return fine_next, totals.reshape(group_fines), coarse_next
 
     placed = (P(("dp", "own"), None), P(("dp", "own")), P("dp", None), P("dp", None))

time: 129 us -> 117 us (0.907)
  local copies, waits for them, and re-layouts: 6.81 us -> 0 us
  Pallas kernels: 120 us -> 116 us
    pallas_call x1, Pallas kernels: 120 us -> 111 us  [on_device(): pl.pallas_call(functools.partial(kernel, n_x, n_y, n_z), out_shape=(jax.S...]
    unnamed x11 -> x0, local copies, waits for them, and re-layouts: 6.81 us -> none
    pallas_call x0 -> x1, Pallas kernels: none -> 4.45 us  [on_device(): pl.pallas_call(functools.partial(arrange, n_y), grid=(n_x,), out_shape=(j...]
where the time goes in v2:
time: 117 us
  Pallas kernels  116 us (99%)
    pallas_call x1, Pallas kernels, on_device(): pl.pallas_call(functools.partial(kernel, n_x, n_y, n_z), out_shape=(jax.S...  111 us
    pallas_call x1, Pallas kernels, on_device(): pl.pallas_call(functools.partial(arrange, n_y), grid=(n_x,), out_shape=(j...  4.45 us

profile of v2, /device:TPU:1, one launch (start us, length us, event | category | flops | bytes accessed | tf_op | source)
XLA Modules:
  0.0 116.6 jit_solution(3481954236735401544)
XLA Ops:
  0.6 111.5 %shard_map.67 = (f32[256,256]{1,0:T(8,128)}, f32[1,256]{1,0:T(1,128)}, bf16[2,4,8,16,1024]{4,3,2,1,0:T(8,128)(2,1)}) custom-call(bf16[128,4096]{1,0:T(8,128)(2,1)} %emb_hbm.1, s32[1,1,128]{2,1,0:T(1,128)} %bitcast.2, bf16[256,4096]{1,0:T(8,128)(2,1)} %fines_hbm.1, bf16[4,4096]{1,0:T(4,128)(2,1)} %coarse_hbm.1), custom_call_target="tpu_custom_call" | custom-call | tf_op jit(solution)/shard_map/pallas_call | solution.py:469
  112.1 4.5 %shard_map.68 = (f32[256,256]{1,0:T(8,128)}, f32[1,256]{1,0:T(1,128)}, bf16[256,4096]{1,0:T(8,128)(2,1)}) custom-call(bf16[2,4,8,16,1024]{4,3,2,1,0:T(8,128)(2,1)} %get-tuple-element.9.blocks, f32[256,256]{1,0:T(8,128)} %get-tuple-element.10.fine, f32[1,256]{1,0:T(1,128)} %get-tuple-element.11.tot), custom_call_target="tpu_custom_call" | custom-call | tf_op jit(solution)/shard_map/pallas_call | solution.py:520

commit v3 on v2

--- a/solution.py
+++ b/solution.py
@@ -15,7 +15,7 @@
 PARTS = 4
 BLK = CAP * PARTS
 N_X = 4
-SUBS = 2
+SUBS = 4
 F32 = jnp.float32
 BF16 = jnp.bfloat16
 
@@ -36,9 +36,9 @@
     ids_hbm,
     fines_hbm,
     coarse_hbm,
-    fine_hbm,
-    tot_hbm,
-    blocks_hbm,
+    fine_out,
+    tot_out,
+    coarse_out,
     emb,
     ids_ref,
     fines,
@@ -56,10 +56,7 @@
     cpart,
     cbox,
     folded,
-    mine_y,
     gath,
-    fine_out,
-    tot_out,
     load_sem,
     ids_send,
     ids_recv,
@@ -72,7 +69,6 @@
     y_recv,
     x_recv,
     core_recv,
-    store_sem,
 ):
     n_dp = 2 * n_x * n_y
     rows, width = emb_hbm.shape
@@ -99,10 +95,8 @@
         )
         copy.start()
 
-    def z_peers(body):
-        @pl.loop(1, n_z)
-        def _(k):
-            body(lax.rem(z + k, n_z))
+    def far_first(n):
+        return sorted(range(1, n), key=lambda k: -min(k, n - k))
 
     barrier = pltpu.get_barrier_semaphore()
 
@@ -133,6 +127,20 @@
         pl.semaphore_signal(
             barrier, inc=1, device_id={"own": lax.rem(z + k, n_z)}, device_id_type=MESH
         )
+
+    quarter_from = (1, n_z - 1, 2)
+    quarter_to = (n_z - 1, 1, n_z - 2)
+
+    @pl.loop(1, n_y)
+    def _(k):
+        dest = (x * n_y + lax.rem(y + k, n_y)) * 2 + core
+        for d in quarter_from:
+            pl.semaphore_signal(
+                barrier,
+                inc=1,
+                device_id={"dp": dest, "own": lax.rem(z + d, n_z)},
+                device_id_type=MESH,
+            )
 
     load_ids.wait()
     ids = ids_ref[0]
@@ -157,17 +165,21 @@
     ids_box[n_dp - 2] = ids
     for load in loads[:PARTS]:
         load.wait()
-    pl.semaphore_wait(barrier, n_dp - 1 + n_z - 1)
-
     chunk = n_y * BLK
 
-    @pl.loop(0, 2 * n_x)
-    def _(jc):
+    def build(jc):
         base = pl.multiple_of(jc * chunk, chunk)
         hot = (iota((chunk, PARTS * rows), 0) + base == target).astype(F32).astype(BF16)
         outbox[pl.ds(base, chunk), :] = jnp.dot(
             hot, emb[...], preferred_element_type=F32
         ).astype(BF16)
+
+    build(0)
+    pl.semaphore_wait(barrier, n_dp - 1 + n_z - 1 + 3 * (n_y - 1))
+
+    @pl.loop(0, 2 * n_x)
+    def _(jc):
+        base = pl.multiple_of(jc * chunk, chunk)
         dest_core = lax.div(jc, n_x)
         at_x = lax.rem(jc, n_x)
         dest_x = lax.rem(x + at_x + 1, n_x)
@@ -193,6 +205,10 @@
                 @pl.when(mine)
                 def _():
                     pltpu.make_async_copy(src, dst, a2a_recv.at[at_x]).start()
+
+        @pl.when(jc + 1 < 2 * n_x)
+        def _():
+            build(jc + 1)
 
     loads[PARTS].wait()
     loads[PARTS + 1].wait()
@@ -222,8 +238,8 @@
     rows_b = src_b * CAP
     out_row = iota((src_b * BLK, src_b * BLK), 0)
     in_row = iota((src_b * BLK, src_b * BLK), 1)
-    quarter = lax.div(out_row, rows_b)
-    within = lax.rem(out_row, rows_b)
+    quarter = out_row >> (rows_b.bit_length() - 1)
+    within = out_row & (rows_b - 1)
     perm = (in_row == (within >> 2) * BLK + quarter * CAP + (within & 3)).astype(F32).astype(BF16)
     for b in range(n_x):
         arrived = inbox.at[pl.ds(b * src_b * BLK, src_b * BLK)]
@@ -255,9 +271,9 @@
     probs = expo / jnp.sum(expo, axis=1, keepdims=True) * valid
 
     tot_box[z] = jnp.sum(probs, axis=0, keepdims=True)
-    z_peers(
-        lambda to: send(tot_box.at[z], tot_box.at[z], st_send.at[0], st_recv.at[0], own=to)
-    )
+    for d in far_first(n_z):
+        to = lax.rem(z + d, n_z)
+        send(tot_box.at[z], tot_box.at[z], st_send.at[0], st_recv.at[0], own=to)
 
     weights = jnp.transpose(probs).astype(BF16)
 
@@ -316,8 +332,6 @@
     for k in range(1, n_z):
         totals = totals + tot_box[k]
     tot_out[...] = totals
-    store_tot = pltpu.make_async_copy(tot_out, tot_hbm, store_sem.at[0])
-    store_tot.start()
     tot_col = jnp.sum(jnp.where(eye_f, totals, 0.0), axis=1, keepdims=True)
     share = 1.0 / (4.0 + tot_col)
     mean_share = share * (1.0 / FINE_PER)
@@ -331,7 +345,7 @@
         cpart[p] = folded[...].astype(BF16)
     my_quarter = lax.rem(z, PARTS)
     cbox[z] = cpart[my_quarter]
-    for d in range(1, n_z):
+    for d in far_first(n_z):
         to = lax.rem(z + d, n_z)
         send(cpart.at[lax.rem(to, PARTS)], cbox.at[z], st_send.at[1], st_recv.at[1], own=to)
     for k in range(wide):
@@ -347,54 +361,35 @@
     for k in range(n_z):
         piece = piece + cbox[k].astype(F32)
     quarter_cols = pl.ds(pl.multiple_of(my_quarter * cols, 128), cols)
-    mine = mine_y.at[:, quarter_cols]
+    mine = gath.at[core, x, y, :, quarter_cols]
     mine[...] = piece.astype(BF16)
-    for d in (1, n_z - 1, n_z - 2):
-        send(mine, mine, st_send.at[2], st_recv.at[2], own=lax.rem(z + d, n_z))
+    for k in [*far_first(n_y), 0]:
+        dest = (x * n_y + lax.rem(y + n_y - k, n_y)) * 2 + core
+        sem = st_send.at[2 if k else 5]
+        if k:
+            send(mine, mine, sem, y_recv.at[k], dp=dest)
+        for d in quarter_to:
+            send(mine, mine, sem, y_recv.at[k], dp=dest, own=lax.rem(z + d, n_z))
+
     ring_step(5)
-    drain(mine_y.at[:, pl.ds(0, 3 * cols)], st_recv.at[2])
-
     other = me + 1 - 2 * core
-    gath[core, x, y] = mine_y[...]
-    near = sorted(range(1, n_y), key=lambda k: min(k, n_y - k))
-
-    def along_x(at_y):
-        block = gath.at[core, x, at_y]
-        for k in range(1, n_x):
-            dest = (lax.rem(x + k, n_x) * n_y + y) * 2 + core
-            send(block, block, st_send.at[5], x_recv.at[k], dp=dest)
-
-    for k in near:
-        dest = (x * n_y + lax.rem(y + n_y - k, n_y)) * 2 + core
-        block = gath.at[core, x, y]
-        send(block, block, st_send.at[3], y_recv.at[k], dp=dest)
-    along_x(y)
+    for k in [0, *reversed(far_first(n_y))]:
+        block = gath.at[core, x, lax.rem(y + k, n_y)]
+        drain(block.at[:, pl.ds(0, (PARTS if k else PARTS - 1) * cols)], y_recv.at[k])
+        for kx in far_first(n_x):
+            dest = (lax.rem(x + kx, n_x) * n_y + y) * 2 + core
+            send(block, block, st_send.at[3], x_recv.at[kx], dp=dest)
     ring_step(6)
-    for k in near:
-        at_y = lax.rem(y + k, n_y)
-        drain(gath.at[core, x, at_y], y_recv.at[k])
-        along_x(at_y)
 
     def pass_on(k):
         column = gath.at[core, lax.rem(x - k + n_x, n_x)]
         send(column, column, st_send.at[4], core_recv.at[k], dp=other)
-        store_column(core, k, k)
-
-    stores = []
-
-    def store_column(of_core, k, sem):
-        at = lax.rem(x - k + n_x, n_x)
-        stores.append(
-            pltpu.make_async_copy(
-                gath.at[of_core, at], blocks_hbm.at[of_core, at], store_sem.at[2 + sem]
-            )
-        )
-        stores[-1].start()
 
     pass_on(0)
     for t in range(7, steps[0]):
         ring_step(t)
-    for k in range(1, n_x):
+    near_x = [0, *reversed(far_first(n_x))]
+    for k in near_x[1:]:
         drain(gath.at[core, lax.rem(x - k + n_x, n_x)], x_recv.at[k])
         pass_on(k)
 
@@ -408,49 +403,53 @@
     my_cols = pl.ds(pl.multiple_of(z * cols, 128), cols)
     fine_out[...] = (4.0 * fines[:, my_cols].astype(F32) + sums) * share
 
-    store_fine = pltpu.make_async_copy(fine_out, fine_hbm, store_sem.at[1])
-    store_fine.start()
-
-    for k in range(n_x):
+
+    blk = wide * CLU_DEV
+    rows_x = 2 * n_y * CLU_DEV
+    out_row = iota((rows_x * wide, rows_x * wide), 0)
+    in_row = iota((rows_x * wide, rows_x * wide), 1)
+    within = out_row & (rows_x - 1)
+    from_block = ((within >> 2) & 1) * n_y + (within >> 3)
+    at_cols = out_row >> (rows_x.bit_length() - 1)
+    from_row = from_block * blk + at_cols * CLU_DEV + (within & 3)
+    perm_x = (in_row == from_row).astype(F32).astype(BF16)
+    for k in near_x:
         at = lax.rem(x - k + n_x, n_x)
         drain(gath.at[1 - core, at], core_recv.at[k])
-        store_column(1 - core, k, n_x + k)
-    for store in [store_tot, store_fine, *stores]:
-        store.wait()
+        both = jnp.concatenate([gath[c, at, i] for c in range(2) for i in range(n_y)], axis=0)
+        gathered = jnp.dot(perm_x, both, preferred_element_type=F32).astype(BF16)
+        at_rows = pl.ds(pl.multiple_of(at * rows_x, rows_x), rows_x)
+        for p in range(PARTS):
+            for j in range(wide):
+                coarse_out[at_rows, pl.ds(p * part + j * cols, cols)] = gathered[
+                    j * rows_x : (j + 1) * rows_x, p * cols : (p + 1) * cols
+                ]
+
     drain(ids_box.at[pl.ds(0, n_dp - 1)], ids_send)
     drain(outbox.at[pl.ds(0, (n_dp - 1) * BLK)], a2a_send)
     drain(tot_box.at[pl.ds(0, n_z - 1)], st_send.at[0])
     drain(cbox.at[pl.ds(0, n_z - 1)], st_send.at[1])
-    drain(mine_y.at[:, pl.ds(0, 3 * cols)], st_send.at[2])
-    drain(gath.at[0, 0, pl.ds(0, n_y - 1)], st_send.at[3])
+    drain(gath.at[0, 0, pl.ds(0, n_y - 1)], st_send.at[2])
+    drain(gath.at[0, 0, 0, :, pl.ds(0, (PARTS - 1) * cols)], st_send.at[5])
+    drain(gath.at[0, pl.ds(0, n_x - 1)], st_send.at[3])
     drain(gath.at[0], st_send.at[4])
-    drain(gath.at[0, pl.ds(0, n_x - 1)], st_send.at[5])
     for way in range(2):
         for t in range(steps[way]):
             for s in range(SUBS):
                 drain(rs_buf.at[way, t, pl.ds(s * sub, sub)], rs_send.at[way, t, s])
 
 
-def arrange(n_y, blocks, fine, tot, fine_out, tot_out, coarse_out):
-    blk, width = blocks.shape[-2:]
-    wide = blk // CLU_DEV
-    cols = width // PARTS
-    rows_x = 2 * n_y * CLU_DEV
-    out_row = iota((rows_x * wide, rows_x * wide), 0)
-    in_row = iota((rows_x * wide, rows_x * wide), 1)
-    within = lax.rem(out_row, rows_x)
-    from_block = ((within >> 2) & 1) * n_y + lax.div(within, 2 * CLU_DEV)
-    from_row = from_block * blk + lax.div(out_row, rows_x) * CLU_DEV + (within & 3)
-    perm = (in_row == from_row).astype(F32).astype(BF16)
-    both = jnp.concatenate([blocks[c, 0, i] for c in range(2) for i in range(n_y)], axis=0)
-    rows = jnp.dot(perm, both, preferred_element_type=F32).astype(BF16)
-    for p in range(PARTS):
-        for j in range(wide):
-            coarse_out[:, pl.ds((p * wide + j) * cols, cols)] = rows[
-                j * rows_x : (j + 1) * rows_x, p * cols : (p + 1) * cols
-            ]
-    fine_out[...] = fine[...]
-    tot_out[...] = tot[...]
+def store(fine, tot, coarse, fine_out, tot_out, coarse_out, sems):
+    step = coarse.shape[0] // 4
+    copies = [(fine, fine_out), (tot, tot_out)]
+    for i in range(4):
+        at = pl.ds(i * step, step)
+        copies.append((coarse.at[at], coarse_out.at[at]))
+    started = [pltpu.make_async_copy(a, b, sems.at[i]) for i, (a, b) in enumerate(copies)]
+    for copy in started:
+        copy.start()
+    for copy in started:
+        copy.wait()
 
 
 def solution(mesh):
@@ -464,17 +463,20 @@
         cols = width // n_z
         part = width // PARTS
         blk = part // cols * CLU_DEV
-        hbm = pl.BlockSpec(memory_space=pl.ANY)
+        hbm = pl.BlockSpec(memory_space=pltpu.HBM)
+        vmem = pl.BlockSpec(memory_space=pltpu.VMEM)
         dma = pltpu.SemaphoreType.DMA
-        fine_next, totals, blocks = pl.pallas_call(
+        operands = (embeddings, coarse_ids.reshape(1, 1, rows), fine_cents, coarse_prev)
+        operands = [pltpu.with_memory_space_constraint(a, pltpu.HBM) for a in operands]
+        results = pl.pallas_call(
             functools.partial(kernel, n_x, n_y, n_z),
             out_shape=(
-                jax.ShapeDtypeStruct((group_fines, cols), F32),
-                jax.ShapeDtypeStruct((1, group_fines), F32),
-                jax.ShapeDtypeStruct((2, n_x, n_y, blk, PARTS * cols), BF16),
+                pltpu.VMEM((group_fines, cols), F32),
+                pltpu.VMEM((1, group_fines), F32),
+                pltpu.VMEM((n_dp * CLU_DEV, width), BF16),
             ),
             in_specs=[hbm, hbm, hbm, hbm],
-            out_specs=(hbm, hbm, hbm),
+            out_specs=(vmem, vmem, vmem),
             scratch_shapes=[
                 pltpu.VMEM((PARTS * rows, part), BF16),
                 pltpu.VMEM((1, 1, rows), jnp.int32),
@@ -493,10 +495,7 @@
                 pltpu.VMEM((PARTS, blk, cols), BF16),
                 pltpu.VMEM((n_z, blk, cols), BF16),
                 pltpu.VMEM((blk, cols), F32),
-                pltpu.VMEM((blk, PARTS * cols), BF16),
                 pltpu.VMEM((2, n_x, n_y, blk, PARTS * cols), BF16),
-                pltpu.VMEM((group_fines, cols), F32),
-                pltpu.VMEM((1, group_fines), F32),
                 dma((PARTS + 3,)),
                 dma(()),
                 dma(()),
@@ -505,38 +504,23 @@
                 dma((2, max(n_z // 2, 1), SUBS)),
                 dma((2, max(n_z // 2, 1), SUBS)),
                 dma((6,)),
-                dma((3,)),
+                dma((2,)),
                 dma((n_y,)),
                 dma((n_x,)),
                 dma((n_x,)),
-                dma((2 + 2 * n_x,)),
             ],
             compiler_params=pltpu.CompilerParams(
-                collective_id=0, has_side_effects=True, vmem_limit_bytes=60 * 2**20
+                collective_id=0, has_side_effects=True, vmem_limit_bytes=40 * 2**20
             ),
-        )(embeddings, coarse_ids.reshape(1, 1, rows), fine_cents, coarse_prev)
-        whole_fine = pl.BlockSpec((group_fines, cols), lambda i: (0, 0))
-        whole_tot = pl.BlockSpec((1, group_fines), lambda i: (0, 0))
+        )(*operands)
         fine_next, totals, coarse_next = pl.pallas_call(
-            functools.partial(arrange, n_y),
-            grid=(n_x,),
-            out_shape=(
-                jax.ShapeDtypeStruct((group_fines, cols), F32),
-                jax.ShapeDtypeStruct((1, group_fines), F32),
-                jax.ShapeDtypeStruct((n_dp * CLU_DEV, width), BF16),
-            ),
-            in_specs=[
-                pl.BlockSpec((2, 1, n_y, blk, PARTS * cols), lambda i: (0, i, 0, 0, 0)),
-                whole_fine,
-                whole_tot,
-            ],
-            out_specs=(
-                whole_fine,
-                whole_tot,
-                pl.BlockSpec((2 * n_y * CLU_DEV, width), lambda i: (i, 0)),
-            ),
-            compiler_params=pltpu.CompilerParams(vmem_limit_bytes=60 * 2**20),
-        )(blocks, fine_next, totals)
+            store,
+            out_shape=tuple(jax.ShapeDtypeStruct(a.shape, a.dtype) for a in results),
+            in_specs=[vmem, vmem, vmem],
+            out_specs=(hbm, hbm, hbm),
+            scratch_shapes=[dma((6,))],
+            compiler_params=pltpu.CompilerParams(vmem_limit_bytes=8 * 2**20),
+        )(*results)
         return fine_next, totals.reshape(group_fines), coarse_next
 
     placed = (P(("dp", "own"), None), P(("dp", "own")), P("dp", None), P("dp", None))

time: 117 us -> 112 us (0.957)
  Pallas kernels: 116 us -> 111 us
    pallas_call x2, Pallas kernels: 116 us -> 111 us  [the longest x1 110 us: on_device(): pl.pallas_call(functools.partial(kernel, n_x, n_y, n_z), out_shape=(pltpu...]
where the time goes in v3:
time: 112 us
  Pallas kernels  111 us (99%)
    pallas_call x1, Pallas kernels, on_device(): pl.pallas_call(functools.partial(kernel, n_x, n_y, n_z), out_shape=(pltpu...  110 us

profile of v3, /device:TPU:1, one launch (start us, length us, event | category | flops | bytes accessed | tf_op | source)
XLA Modules:
  0.0 111.9 jit_solution(6363253503243346964)
XLA Ops:
  0.6 109.8 %shard_map.67 = (f32[256,256]{1,0:T(8,128)S(1)}, f32[1,256]{1,0:T(1,128)S(1)}, bf16[256,4096]{1,0:T(8,128)(2,1)S(1)}) custom-call(bf16[128,4096]{1,0:T(8,128)(2,1)} %emb_hbm.1, s32[1,1,128]{2,1,0:T(1,128)} %bitcast.2, bf16[256,4096]{1,0:T(8,128)(2,1)} %fines_hbm.1, bf16[4,4096]{1,0:T(4,128)(2,1)} %coarse_hbm.1), custom_call_target="tpu_custom_call" | custom-call | tf_op jit(solution)/shard_map/pallas_call | solution.py:471
  110.4 1.5 %shard_map.68 = (f32[256,256]{1,0:T(8,128)}, f32[1,256]{1,0:T(1,128)}, bf16[256,4096]{1,0:T(8,128)(2,1)}) custom-call(f32[256,256]{1,0:T(8,128)S(1)} %get-tuple-element.9.fine, f32[1,256]{1,0:T(1,128)S(1)} %get-tuple-element.10.tot, bf16[256,4096]{1,0:T(8,128)(2,1)S(1)} %get-tuple-element.11.coarse), custom_call_target="tpu_custom_call" | custom-call | tf_op jit(solution)/shard_map/pallas_call | solution.py:516

commit v4 on v3

--- a/solution.py
+++ b/solution.py
@@ -339,15 +339,17 @@
     def cluster_sum(value):
         return jnp.sum(value.reshape(CLU_DEV, FINE_PER, cols), axis=1)
 
-    for p in range(PARTS):
+    my_quarter = lax.rem(z, PARTS)
+    for i in (0, 3, 1, 2):
+        q = lax.rem(z + i, PARTS)
         for k in range(wide):
-            folded[pl.ds(k * CLU_DEV, CLU_DEV), :] = cluster_sum(stats[p * wide + k] * mean_share)
-        cpart[p] = folded[...].astype(BF16)
-    my_quarter = lax.rem(z, PARTS)
+            folded[pl.ds(k * CLU_DEV, CLU_DEV), :] = cluster_sum(stats[q * wide + k] * mean_share)
+        cpart[q] = folded[...].astype(BF16)
+        for d in far_first(n_z):
+            if d % PARTS == i:
+                to = lax.rem(z + d, n_z)
+                send(cpart.at[q], cbox.at[z], st_send.at[1], st_recv.at[1], own=to)
     cbox[z] = cpart[my_quarter]
-    for d in far_first(n_z):
-        to = lax.rem(z + d, n_z)
-        send(cpart.at[lax.rem(to, PARTS)], cbox.at[z], st_send.at[1], st_recv.at[1], own=to)
     for k in range(wide):
         at = pl.ds(pl.multiple_of(my_quarter * part + k * cols, 128), cols)
         folded[pl.ds(k * CLU_DEV, CLU_DEV), :] = coarse_ref[:, at].astype(F32) + cluster_sum(
@@ -388,10 +390,29 @@
     pass_on(0)
     for t in range(7, steps[0]):
         ring_step(t)
-    near_x = [0, *reversed(far_first(n_x))]
-    for k in near_x[1:]:
-        drain(gath.at[core, lax.rem(x - k + n_x, n_x)], x_recv.at[k])
-        pass_on(k)
+    blk = wide * CLU_DEV
+    rows_x = 2 * n_y * CLU_DEV
+    out_row = iota((rows_x * wide, rows_x * wide), 0)
+    in_row = iota((rows_x * wide, rows_x * wide), 1)
+    within = out_row & (rows_x - 1)
+    from_block = ((within >> 2) & 1) * n_y + (within >> 3)
+    at_cols = out_row >> (rows_x.bit_length() - 1)
+    from_row = from_block * blk + at_cols * CLU_DEV + (within & 3)
+    perm_x = (in_row == from_row).astype(F32).astype(BF16)
+    for k in [0, *reversed(far_first(n_x))]:
+        at = lax.rem(x - k + n_x, n_x)
+        if k:
+            drain(gath.at[core, at], x_recv.at[k])
+            pass_on(k)
+        drain(gath.at[1 - core, at], core_recv.at[k])
+        both = jnp.concatenate([gath[c, at, i] for c in range(2) for i in range(n_y)], axis=0)
+        gathered = jnp.dot(perm_x, both, preferred_element_type=F32).astype(BF16)
+        at_rows = pl.ds(pl.multiple_of(at * rows_x, rows_x), rows_x)
+        for p in range(PARTS):
+            for j in range(wide):
+                coarse_out[at_rows, pl.ds(p * part + j * cols, cols)] = gathered[
+                    j * rows_x : (j + 1) * rows_x, p * cols : (p + 1) * cols
+                ]
 
     sums = stats[z]
     for way in range(2):
@@ -402,28 +423,6 @@
             sums = sums + rs_buf[way, steps[way] - 1].astype(F32)
     my_cols = pl.ds(pl.multiple_of(z * cols, 128), cols)
     fine_out[...] = (4.0 * fines[:, my_cols].astype(F32) + sums) * share
-
-
-    blk = wide * CLU_DEV
-    rows_x = 2 * n_y * CLU_DEV
-    out_row = iota((rows_x * wide, rows_x * wide), 0)
-    in_row = iota((rows_x * wide, rows_x * wide), 1)
-    within = out_row & (rows_x - 1)
-    from_block = ((within >> 2) & 1) * n_y + (within >> 3)
-    at_cols = out_row >> (rows_x.bit_length() - 1)
-    from_row = from_block * blk + at_cols * CLU_DEV + (within & 3)
-    perm_x = (in_row == from_row).astype(F32).astype(BF16)
-    for k in near_x:
-        at = lax.rem(x - k + n_x, n_x)
-        drain(gath.at[1 - core, at], core_recv.at[k])
-        both = jnp.concatenate([gath[c, at, i] for c in range(2) for i in range(n_y)], axis=0)
-        gathered = jnp.dot(perm_x, both, preferred_element_type=F32).astype(BF16)
-        at_rows = pl.ds(pl.multiple_of(at * rows_x, rows_x), rows_x)
-        for p in range(PARTS):
-            for j in range(wide):
-                coarse_out[at_rows, pl.ds(p * part + j * cols, cols)] = gathered[
-                    j * rows_x : (j + 1) * rows_x, p * cols : (p + 1) * cols
-                ]
 
     drain(ids_box.at[pl.ds(0, n_dp - 1)], ids_send)
     drain(outbox.at[pl.ds(0, (n_dp - 1) * BLK)], a2a_send)

time: 112 us -> 113 us (level)
    pallas_call x1, Pallas kernels: 110 us -> 111 us  [on_device(): pl.pallas_call(functools.partial(kernel, n_x, n_y, n_z), out_shape=(pltpu...]
where the time goes in v4:
time: 113 us
  Pallas kernels  112 us (99%)
    pallas_call x1, Pallas kernels, on_device(): pl.pallas_call(functools.partial(kernel, n_x, n_y, n_z), out_shape=(pltpu...  111 us

profile of v4, /device:TPU:1, one launch (start us, length us, event | category | flops | bytes accessed | tf_op | source)
XLA Modules:
  0.0 113.1 jit_solution(7177427092371596615)
XLA Ops:
  0.6 111.0 %shard_map.67 = (f32[256,256]{1,0:T(8,128)S(1)}, f32[1,256]{1,0:T(1,128)S(1)}, bf16[256,4096]{1,0:T(8,128)(2,1)S(1)}) custom-call(bf16[128,4096]{1,0:T(8,128)(2,1)} %emb_hbm.1, s32[1,1,128]{2,1,0:T(1,128)} %bitcast.2, bf16[256,4096]{1,0:T(8,128)(2,1)} %fines_hbm.1, bf16[4,4096]{1,0:T(4,128)(2,1)} %coarse_hbm.1), custom_call_target="tpu_custom_call" | custom-call | tf_op jit(solution)/shard_map/pallas_call | solution.py:470
  111.6 1.5 %shard_map.68 = (f32[256,256]{1,0:T(8,128)}, f32[1,256]{1,0:T(1,128)}, bf16[256,4096]{1,0:T(8,128)(2,1)}) custom-call(f32[256,256]{1,0:T(8,128)S(1)} %get-tuple-element.9.fine, f32[1,256]{1,0:T(1,128)S(1)} %get-tuple-element.10.tot, bf16[256,4096]{1,0:T(8,128)(2,1)S(1)} %get-tuple-element.11.coarse), custom_call_target="tpu_custom_call" | custom-call | tf_op jit(solution)/shard_map/pallas_call | solution.py:515
